TPU v7x, 32 devices: a whole 2x2x4 slice. The times are simulated.
32 devices in a mesh: groups: 1, tensor: 32 (over z, y, x, core).
Axes of the slice: x: 2, y: 2, z: 4, core: 2. Of those that a mesh axis runs over, the one named last changes fastest.
Arguments:
- query_grads: bfloat16 [2, 4096, 16384], P('groups', 'tensor'), may hold values from -0.0007324219 to 0.0007324219
- eigen_values: float32 [4096, 16384], P('groups', 'tensor'), may hold values from 0.1 to 10
- act_basis: bfloat16 [128, 128, 128], P(('groups', 'tensor')), may hold values from -0.5 to 0.5
- grad_basis: bfloat16 [4096, 256], P(('groups', 'tensor')), may hold values from -0.375 to 0.375
- activations: bfloat16 [256, 16384], P(('groups', 'tensor')), may hold values from -6 to 6
- cotangents: bfloat16 [256, 4096], P(('groups', 'tensor')), may hold values from -6 to 6
- block_tokens: int32 [256], P('groups'), may hold values from 0 to 255, each once
- pair_query: int32 [24], P('groups'), may hold values from 0 to 1
- pair_block: int32 [24], P('groups'), may hold values from 0 to 1
Outputs:
- scores: float32 [24, 128], P('groups')
Inputs may be any that keep to these rules, and one draw needn't show every extreme that they name: `block_tokens`: a permutation of the training tokens.
All inputs are finite; a program needn't handle non-finite values.
Results may differ from a plain program's by a relative error of at most 0.005.
Values may be sent and summed in bfloat16 or wider, within the bound.
A program may use at most 128 MiB of HBM per device.

v0:
```python
import jax
import jax.numpy as jnp
from jax import lax
from jax.sharding import PartitionSpec as P

BLOCK = 128


damping = 0.1


def rotate_rows(rows, grad_blocks):
    row_count = rows.shape[0]
    nblocks = grad_blocks.shape[0]
    block_width = grad_blocks.shape[1]
    reshaped = rows.reshape(row_count, nblocks, block_width)
    turned = jnp.einsum("tcg,cgh->tch", reshaped, grad_blocks, preferred_element_type=jnp.float32)
    return turned.astype(jnp.bfloat16).reshape(row_count, nblocks * block_width)


def per_device(
    query_grads,
    eigen_values,
    act_basis,
    grad_basis,
    activations,
    cotangents,
    block_tokens,
    pair_query,
    pair_block,
):
    grad_full = lax.all_gather(grad_basis, "tensor", axis=0, tiled=True)
    block_width = grad_full.shape[1]
    model_cols = grad_full.shape[0]
    grad_blocks = grad_full.reshape(model_cols // block_width, block_width, block_width)
    act_local = lax.all_to_all(activations, "tensor", split_axis=1, concat_axis=0, tiled=True)
    tokens_all = act_local.shape[0]
    slice_cols = act_local.shape[1]
    owned_blocks = act_basis.shape[0]
    act_size = act_basis.shape[1]
    act_rot = jnp.einsum(
        "tkb,kbc->tkc",
        act_local.reshape(tokens_all, owned_blocks, act_size),
        act_basis,
        preferred_element_type=jnp.float32,
    )
    act_rot = act_rot.astype(jnp.bfloat16).reshape(tokens_all, slice_cols)
    cot_mine = rotate_rows(cotangents, grad_blocks)
    cot_rot = lax.all_gather(cot_mine, "tensor", axis=0, tiled=True)
    query_piece = lax.all_to_all(query_grads, "tensor", split_axis=2, concat_axis=1, tiled=True)
    number = query_piece.shape[0]
    turned = jnp.einsum(
        "nokb,kbc->nokc",
        query_piece.reshape(number, model_cols, owned_blocks, act_size),
        act_basis,
        preferred_element_type=jnp.float32,
    ).astype(jnp.bfloat16)
    turned = turned.reshape(number, model_cols // block_width, block_width, slice_cols)
    rotated = jnp.einsum("cgh,ncgf->nchf", grad_blocks, turned, preferred_element_type=jnp.float32)
    rotated = rotated.reshape(number, model_cols, slice_cols)
    precond = (rotated / (eigen_values + damping)).astype(jnp.bfloat16)
    blocks = block_tokens.reshape(-1, BLOCK)
    act_wide = act_rot.astype(jnp.float32)

    def score_query(matrix):
        values = jnp.dot(cot_rot, matrix, preferred_element_type=jnp.float32)
        return jnp.sum(values * act_wide, axis=1)

    totals = lax.map(score_query, precond)
    picked = jnp.take(totals, pair_query, axis=0)
    token_ids = jnp.take(blocks, pair_block, axis=0)
    partial_value = jnp.take_along_axis(picked, token_ids, axis=1)
    return lax.psum(partial_value, "tensor")


def solution(mesh):
    return jax.shard_map(
        per_device,
        mesh=mesh,
        in_specs=(
            P("groups", "tensor", None),
            P("groups", "tensor"),
            P(("groups", "tensor"), None, None),
            P(("groups", "tensor"), None),
            P(("groups", "tensor"), None),
            P(("groups", "tensor"), None),
            P("groups"),
            P("groups"),
            P("groups"),
        ),
        out_specs=P("groups", None),
        check_vma=False,
    )
```

profile of v0, /device:TPU:0, one launch (start us, length us, event | category | flops | bytes accessed | tf_op | source)
XLA Modules:
  0.0 405.5 jit_solution(5121336644992953163)
XLA Ops:
  6.5 7.3 %all-to-all-start.1 = ((bf16[8,32,512]{2,0,1:T(8,128)(2,1)}), bf16[8,32,512]{2,0,1:T(8,128)(2,1)S(1)}, u32[]{:S(2)}, u32[]{:S(2)}) async-start(bf16[8,32,512]{2,0,1:T(8,128)(2,1)} %bitcast.89), calls=%async_computation.1 | async-start | bytes 524288 | tf_op jit(solution)/shard_map/all_to_all | solution.py:36
  13.8 21.2 %copy.22 = bf16[2,128,16384]{1,0,2:T(2,128)(2,1)} copy(bf16[2,128,16384]{2,1,0:T(8,128)(2,1)} %param.11) | data formatting | bytes 16777216 | tf_op args[0]
  35.0 6.0 %all-to-all-start = ((bf16[2,128,16384]{1,0,2:T(2,128)(2,1)}), bf16[2,128,16384]{1,0,2:T(2,128)(2,1)}, u32[]{:S(2)}, u32[]{:S(2)}) async-start(bf16[2,128,16384]{1,0,2:T(2,128)(2,1)} %copy.22), calls=%async_computation | async-start | bytes 16777216 | tf_op jit(solution)/shard_map/all_to_all | solution.py:50
  41.0 0.0 all-gather.3.cloned.1.call-start
  41.0 0.7 all-gather.3.cloned.1.call-update
  41.7 0.0 all-gather.5.cloned.1.call-start
  41.8 0.6 gather_fusion
  42.5 0.1 fusion.25
  42.5 7.7 %broadcast_add_fusion = f32[4096,512]{1,0:T(8,128)} fusion(f32[4096,512]{1,0:T(8,128)} %param.12), kind=kLoop, calls=%fused_computation.18 | loop fusion | flops 2097152 | bytes 16777216 | tf_op jit(solution)/shard_map/add | solution.py:61
  50.2 0.1 reshape.102
  50.3 0.3 fusion.19
  50.6 91.3 %all-gather.3.cloned.1.call-done = bf16[4096,256]{1,0:T(8,128)(2,1)} async-done(((bf16[128,256]{1,0:T(8,128)(2,1)}), bf16[4096,256]{1,0:T(8,128)(2,1)}) %all-gather.3.cloned.1.call-update) | async-done | bytes 2097168 | tf_op jit(solution)/shard_map/all_gather | solution.py:32
  141.9 2.6 convolution_convert_fusion.1
  144.5 0.0 all-gather.5.cloned.1.call-update
  144.5 101.2 %all-to-all-done = bf16[2,128,16384]{1,0,2:T(2,128)(2,1)} async-done(((bf16[2,128,16384]{1,0,2:T(2,128)(2,1)}), bf16[2,128,16384]{1,0,2:T(2,128)(2,1)}, u32[]{:S(2)}, u32[]{:S(2)}) %all-to-all-start) | async-done | bytes 8388640 | tf_op jit(solution)/shard_map/all_to_all | solution.py:50
  245.7 12.0 %copy.51 = bf16[2,128,32,512]{1,2,3,0:T(8,128)(2,1)} copy(bf16[2,128,32,512]{1,0,3,2:T(2,128)(2,1)} %bitcast.5) | data formatting | bytes 16777216 | tf_op jit(solution)/shard_map/all_to_all | solution.py:50
  257.7 13.4 %reshape.96 = bf16[2,4096,4,128]{1,3,2,0:T(8,128)(2,1)} reshape(bf16[2,32,128,512]{2,1,3,0:T(8,128)(2,1)} %bitcast.81) | data formatting | bytes 16777216 | tf_op jit(solution)/shard_map/reshape | solution.py:54
  271.0 9.0 %convert_bitcast_fusion = bf16[2,4096,4,128]{1,3,0,2:T(8,128)(2,1)} fusion(bf16[2,4096,4,128]{1,3,2,0:T(8,128)(2,1)} %reshape.96, bf16[4,128,128]{2,1,0:T(8,128)(2,1)S(1)} %copy-done), kind=kOutput, calls=%fused_computation.17 | convolution fusion | flops 1077936128 | bytes 16908288 | tf_op jit(solution)/shard_map/nokb,kbc->nokc/dot_general | solution.py:52
  280.0 7.7 %copy.26 = bf16[2,4096,4,128]{1,3,2,0:T(8,128)(2,1)} copy(bf16[2,4096,4,128]{1,3,0,2:T(8,128)(2,1)} %convert_bitcast_fusion) | data formatting | bytes 16777216 | tf_op jit(solution)/shard_map/convert_element_type | solution.py:57
  287.7 9.9 %copy.41 = bf16[128,8,16,256]{3,2,1,0:T(8,128)(2,1)} copy(bf16[128,8,16,256]{3,1,2,0:T(8,128)(2,1)} %bitcast.82) | data formatting | bytes 16777216
  297.6 15.2 %convolution_bitcast_fusion = f32[2,16,256,512]{3,2,0,1:T(8,128)} fusion(bf16[16,256,256,1]{2,1,3,0:T(8,128)(2,1)S(1)} %bitcast.84, bf16[2,16,256,512]{2,1,3,0:T(8,128)(2,1)} %bitcast.80), kind=kOutput, calls=%fused_computation.12 | convolution fusion | flops 2147483648 | bytes 27262976 | tf_op jit(solution)/shard_map/cgh,ncgf->nchf/dot_general | solution.py:59
  312.8 6.8 %copy.29 = f32[2,16,256,512]{3,2,1,0:T(8,128)S(1)} copy(f32[2,16,256,512]{3,2,0,1:T(8,128)} %convolution_bitcast_fusion) | data formatting | bytes 33554432 | tf_op jit(solution)/shard_map/cgh,ncgf->nchf/transpose | solution.py:59
  319.7 8.1 %fusion.13 = bf16[2,4096,512]{2,1,0:T(8,128)(2,1)} fusion(f32[2,16,256,512]{3,2,1,0:T(8,128)S(1)} %copy.29, f32[4096,512]{1,0:T(8,128)} %broadcast_add_fusion), kind=kLoop, calls=%fused_computation.11 | loop fusion | flops 8388608 | bytes 33554432 | tf_op jit(solution)/shard_map/convert_element_type | solution.py:61
  327.8 8.4 %while.10 = (s32[]{:T(128)}, f32[2,256]{1,0:T(2,128)S(1)}, bf16[2,4096,512]{2,1,0:T(8,128)(2,1)}, bf16[256,4096]{1,0:T(8,128)(2,1)}, f32[256,512]{0,1:T(8,128)S(1)}, /*index=5*/s32[]{:T(128)}, s32[]{:T(128)}) while((s32[]{:T(128)}, f32[2,256]{1,0:T(2,128)S(1)}, bf16[2,4096,512]{2,1,0:T(8,128)(2,1)}, bf16[256,4096]{1,0:T(8,128)(2,1)}, ...), condition=%wide.region_2.3_spmd, body=%wide.region_0.2_spmd.sunk | while | flops 1074003712 | bytes 6819409 | solution.py:69
  327.8 4.2 %fusion.36 = f32[256]{0:T(256)S(1)} fusion(f32[256,512]{0,1:T(8,128)S(1)} %get-tuple-element.92, bf16[256,4096]{1,0:T(8,128)(2,1)} %get-tuple-element.91, bf16[2,4096,512]{2,1,0:T(8,128)(2,1)} %get-tuple-element.90, s32[]{:T(128)} %get-tuple-element.81), kind=kOutput, calls=%fused_computation.8.clone.1 | convolution fusion | flops 1074003712 | bytes 6817280 | tf_op jit(solution)/shard_map/while/body/eval_jaxpr/dot_general | solution.py:66
  332.0 4.2 %fusion.36 = f32[256]{0:T(256)S(1)} fusion(f32[256,512]{0,1:T(8,128)S(1)} %get-tuple-element.92, bf16[256,4096]{1,0:T(8,128)(2,1)} %get-tuple-element.91, bf16[2,4096,512]{2,1,0:T(8,128)(2,1)} %get-tuple-element.90, s32[]{:T(128)} %get-tuple-element.81), kind=kOutput, calls=%fused_computation.8.clone.1 | convolution fusion | flops 1074003712 | bytes 6817280 | tf_op jit(solution)/shard_map/while/body/eval_jaxpr/dot_general | solution.py:66
  336.2 0.0 copy-start.1
  336.2 0.6 gather_fusion.1
  336.8 0.1 broadcast_select_fusion
  336.9 24.7 %gather_fusion.2 = f32[3072]{0:T(1024)S(1)} fusion(f32[24,256]{1,0:T(8,128)S(1)} %broadcast_select_fusion, s32[3072]{0:T(1024)S(1)} %fusion.25), kind=kCustom, calls=%fused_computation.2 | custom fusion | bytes 49152 | tf_op jit(solution)/shard_map/jit(take_along_axis)/gather | solution.py:72
  361.6 0.1 bitcast_select_fusion
  361.7 37.0 %psum.7 = f32[24,128]{1,0:T(8,128)} all-reduce(f32[24,128]{1,0:T(8,128)S(1)} %bitcast_select_fusion), channel_id=1, replica_groups=mesh['groups'=1,'tensor'=32] {'tensor'}, use_global_device_ids=true, to_apply=%region_3.4 | all-reduce | flops 3072 | bytes 24576 | tf_op jit(solution)/shard_map/psum | solution.py:73
  (24 shorter events, 0.1 us)
Async XLA Ops:
  6.5 43.8 %copy-start = (bf16[4,128,128]{2,1,0:T(8,128)(2,1)S(1)}, bf16[4,128,128]{2,1,0:T(8,128)(2,1)}, u32[]{:S(2)}) copy-start(bf16[4,128,128]{2,1,0:T(8,128)(2,1)} %param.13) | copy-start | bytes 393220
  6.5 28.5 %all-to-all-start.1 = ((bf16[8,32,512]{2,0,1:T(8,128)(2,1)}), bf16[8,32,512]{2,0,1:T(8,128)(2,1)S(1)}, u32[]{:S(2)}, u32[]{:S(2)}) async-start(bf16[8,32,512]{2,0,1:T(8,128)(2,1)} %bitcast.89), calls=%async_computation.1 | async-start | bytes 524288 | tf_op jit(solution)/shard_map/all_to_all | solution.py:36
  35.0 6.8 %copy-start.6 = (s32[24]{0:T(128)S(1)}, s32[24]{0:T(128)}, u32[]{:S(2)}) copy-start(s32[24]{0:T(128)} %param.19) | copy-start | bytes 292
  35.0 6.8 %copy-start.3 = (s32[256]{0:T(256)S(1)}, s32[256]{0:T(256)}, u32[]{:S(2)}) copy-start(s32[256]{0:T(256)} %param.17) | copy-start | bytes 3076
  35.0 7.4 %copy-start.5 = (s32[24]{0:T(128)S(1)}, s32[24]{0:T(128)}, u32[]{:S(2)}) copy-start(s32[24]{0:T(128)} %param.18) | copy-start | bytes 292
  35.0 210.6 %all-to-all-start = ((bf16[2,128,16384]{1,0,2:T(2,128)(2,1)}), bf16[2,128,16384]{1,0,2:T(2,128)(2,1)}, u32[]{:S(2)}, u32[]{:S(2)}) async-start(bf16[2,128,16384]{1,0,2:T(2,128)(2,1)} %copy.22), calls=%async_computation | async-start | bytes 16777216 | tf_op jit(solution)/shard_map/all_to_all | solution.py:50
  41.0 100.9 %all-gather.3.cloned.1.call-start = ((), (), s32[]{:S(2)}) async-start(), calls=%async_computation.2 | async-start | bytes 2162688 | tf_op jit(solution)/shard_map/all_gather | solution.py:32
  41.7 286.1 %all-gather.5.cloned.1.call-start = ((), (), s32[]{:S(2)}) async-start(), calls=%async_computation.3 | async-start | bytes 2162688 | tf_op jit(solution)/shard_map/all_gather | solution.py:49
  42.5 99.3 %copy-start.4 = (bf16[8,4096]{1,0:T(8,128)(2,1)S(1)}, bf16[8,4096]{1,0:T(8,128)(2,1)}, u32[]{:S(2)}) copy-start(bf16[8,4096]{1,0:T(8,128)(2,1)} %param.16) | copy-start | bytes 196612
  287.7 9.9 %copy-start.2 = (bf16[4096,256]{1,0:T(8,128)(2,1)S(1)}, bf16[4096,256]{1,0:T(8,128)(2,1)}, u32[]{:S(2)}) copy-start(bf16[4096,256]{1,0:T(8,128)(2,1)} %all-gather.3.cloned.1.call-done) | copy-start | bytes 6291460
  336.2 62.5 %copy-start.1 = (bf16[4,128,128]{2,1,0:T(8,128)(2,1)S(1)}, bf16[4,128,128]{2,1,0:T(8,128)(2,1)}, u32[]{:S(2)}) copy-start(bf16[4,128,128]{2,1,0:T(8,128)(2,1)} %param.13) | copy-start | bytes 393220
Sparse Core Ops, SparseCore 0:
  44.7 97.1 all-gather.2
  144.7 89.0 all-gather.4
where the time goes:
time: 408 us; the launch traced here: 406 us
  waiting for transfers between devices  193 us (47%)
  local copies, waits for them, and re-layouts  97 us (24%)
  blocking collectives  37 us (9%)
  matrix products  35.4 us (9%)
  other arithmetic  16.1 us (4%)
  between operations  13.6 us (3%)
  starting transfers between devices  13.3 us (3%)
    all_to_all x1, waiting for transfers between devices, per_device(): lax.all_to_all(query_grads, 'tensor', split_axis=2, concat_axis=1, tiled=...  101 us
    all_gather x1, waiting for transfers between devices, per_device(): grad_full = lax.all_gather(grad_basis, 'tensor', axis=0, tiled=True)  91.3 us
    psum x1, blocking collectives, per_device(): return lax.psum(partial_value, 'tensor')  37 us
    unnamed x16, local copies, waits for them, and re-layouts  31 us
    gather x1, local copies, waits for them, and re-layouts, per_device(): partial_value = jnp.take_along_axis(picked, token_ids, axis=1)  24.7 us
    dot_general x1, matrix products, per_device(): jnp.einsum('cgh,ncgf->nchf', grad_blocks, turned, preferred_element_type=...  15.2 us
    reshape x1, local copies, waits for them, and re-layouts, per_device(): query_piece.reshape(number, model_cols, owned_blocks, act_size)  13.4 us
    all_to_all x1, local copies, waits for them, and re-layouts, per_device(): lax.all_to_all(query_grads, 'tensor', split_axis=2, concat_axis=1, tiled=...  12 us
  transfers between devices with their start and end apart: 4, of which 2 were waited for; matrix products, arithmetic and copies ran while one was open for 28% of the time, Pallas kernels for 0%

commit v1 on v0

--- a/solution.py
+++ b/solution.py
@@ -18,7 +18,14 @@
     return turned.astype(jnp.bfloat16).reshape(row_count, nblocks * block_width)
 
 
-def per_device(
+def pick_scores(totals, block_tokens, pair_query, pair_block):
+    blocks = block_tokens.reshape(-1, BLOCK)
+    picked = jnp.take(totals, pair_query, axis=0)
+    token_ids = jnp.take(blocks, pair_block, axis=0)
+    return jnp.take_along_axis(picked, token_ids, axis=1)
+
+
+def by_columns(
     query_grads,
     eigen_values,
     act_basis,
@@ -59,7 +66,6 @@
     rotated = jnp.einsum("cgh,ncgf->nchf", grad_blocks, turned, preferred_element_type=jnp.float32)
     rotated = rotated.reshape(number, model_cols, slice_cols)
     precond = (rotated / (eigen_values + damping)).astype(jnp.bfloat16)
-    blocks = block_tokens.reshape(-1, BLOCK)
     act_wide = act_rot.astype(jnp.float32)
 
     def score_query(matrix):
@@ -67,13 +73,69 @@
         return jnp.sum(values * act_wide, axis=1)
 
     totals = lax.map(score_query, precond)
-    picked = jnp.take(totals, pair_query, axis=0)
-    token_ids = jnp.take(blocks, pair_block, axis=0)
-    partial_value = jnp.take_along_axis(picked, token_ids, axis=1)
-    return lax.psum(partial_value, "tensor")
+    return lax.psum(pick_scores(totals, block_tokens, pair_query, pair_block), "tensor")
+
+
+def by_rows(
+    query_grads,
+    eigen_values,
+    act_basis,
+    grad_basis,
+    activations,
+    cotangents,
+    block_tokens,
+    pair_query,
+    pair_block,
+):
+    devices = lax.axis_size("tensor")
+    chips = devices // 2
+    across = [[2 * chip + core for chip in range(chips)] for core in range(2)]
+    pairs = [[2 * chip, 2 * chip + 1] for chip in range(chips)]
+    bf16, f32 = jnp.bfloat16, jnp.float32
+
+    number, rows, hidden = query_grads.shape
+    width = eigen_values.shape[1]
+    wide = 2 * rows
+    half = hidden // 2
+    tokens = activations.shape[0]
+
+    inverse = (1.0 / (eigen_values + damping)).astype(bf16)
+    inverse = lax.all_to_all(inverse, "tensor", 0, 1, axis_index_groups=across, tiled=True)
+    basis = lax.all_gather(act_basis, "tensor", axis=0, axis_index_groups=across, tiled=True)
+    act = activations.reshape(tokens, chips, 2, width)
+    act = lax.all_to_all(act, "tensor", 2, 0, axis_index_groups=pairs, tiled=True)
+    act = act.reshape(2 * tokens, half)
+    act = lax.all_gather(act, "tensor", axis=0, axis_index_groups=across, tiled=True)
+    query = query_grads.reshape(number, rows, chips, 2, width)
+    query = lax.all_to_all(query, "tensor", 3, 1, axis_index_groups=pairs, tiled=True)
+    grad = lax.all_gather(grad_basis, "tensor", axis=0, axis_index_groups=pairs, tiled=True)
+    cot = lax.all_to_all(cotangents, "tensor", 1, 0, axis_index_groups=across, tiled=True)
+    cot = lax.all_gather(cot, "tensor", axis=0, axis_index_groups=pairs)
+    cot = cot.reshape(2, chips, tokens, wide).transpose(1, 0, 2, 3).reshape(devices * tokens, wide)
+
+    cot_rot = jnp.dot(cot, grad, preferred_element_type=f32).astype(bf16)
+    blocks, size, _ = basis.shape
+    act_rot = jnp.einsum("tkb,kbc->tkc", act.reshape(-1, blocks, size), basis, preferred_element_type=f32)
+    act_rot = act_rot.astype(bf16).reshape(-1, half)
+    turned = jnp.einsum(
+        "nokb,kbc->nokc", query.reshape(number, wide, blocks, size), basis, preferred_element_type=f32
+    )
+    turned = turned.astype(bf16).reshape(number, wide, half)
+    rotated = jnp.einsum("gh,ngf->nhf", grad, turned, preferred_element_type=f32)
+    precond = (rotated * inverse.astype(f32)).astype(bf16)
+    values = jnp.einsum("tf,nhf->nth", act_rot, precond, preferred_element_type=f32)
+    totals = jnp.sum(values * cot_rot.astype(f32), axis=2)
+    return pick_scores(lax.psum(totals, "tensor"), block_tokens, pair_query, pair_block)
 
 
 def solution(mesh):
+    devices = mesh.shape["tensor"]
+
+    def per_device(*args):
+        query_grads, grad_basis = args[0], args[3]
+        paired = devices % 2 == 0 and 2 * query_grads.shape[1] == grad_basis.shape[1]
+        return (by_rows if paired else by_columns)(*args)
+
     return jax.shard_map(
         per_device,
         mesh=mesh,

time: 408 us -> 328 us (0.80)
  waiting for transfers between devices: 193 us -> 58.3 us
  blocking collectives: 37 us -> 77.2 us
  matrix products: 35.4 us -> 44.9 us
    all_gather x2, waiting for transfers between devices: 91.3 us -> 21.4 us  [the longest x1 21.4 us: by_rows(): lax.all_gather(act, 'tensor', axis=0, axis_index_groups=across, tiled=True)]
    all_to_all x2 -> x3, waiting for transfers between devices: 101 us -> 36.2 us  [the longest x1 34.8 us: by_rows(): lax.all_to_all(inverse, 'tensor', 0, 1, axis_index_groups=across, tiled=T...]
    all_to_all x0 -> x1, blocking collectives: none -> 18.5 us  [by_rows(): lax.all_to_all(query, 'tensor', 3, 1, axis_index_groups=pairs, tiled=True)]
    unnamed x16 -> x14, local copies, waits for them, and re-layouts: 31 us -> 12.9 us
    psum x1, blocking collectives: 37 us -> 54.7 us  [by_rows(): lax.psum(totals, 'tensor')]
    reshape x2 -> x3, local copies, waits for them, and re-layouts: 13.4 us -> 30.5 us  [the longest x1 14.7 us: by_rows(): query = query_grads.reshape(number, rows, chips, 2, width)]
    convert_element_type x1 -> x3, local copies, waits for them, and re-layouts: 7.7 us -> 17.2 us  [the longest x1 9.28 us: by_rows(): precond = (rotated * inverse.astype(f32)).astype(bf16)]
    dot_general x6 -> x4, matrix products: 35.4 us -> 44.9 us  [the longest x1 25.4 us: by_rows(): jnp.einsum('nokb,kbc->nokc', query.reshape(number, wide, blocks, size), b...]
  transfers between devices with their start and end apart: 4 -> 5, of which waited for: 2 -> 3; matrix products, arithmetic and copies ran while one was open for 28% -> 33% of each run, Pallas kernels for 0% -> 0%
where the time goes in v1:
time: 328 us; the launch traced here: 326 us
  local copies, waits for them, and re-layouts  101 us (31%)
  blocking collectives  77.2 us (24%)
  waiting for transfers between devices  58.3 us (18%)
  matrix products  44.9 us (14%)
  starting transfers between devices  17.3 us (5%)
  other arithmetic  14.2 us (4%)
  between operations  13.5 us (4%)
    psum x1, blocking collectives, by_rows(): lax.psum(totals, 'tensor')  54.7 us
    all_to_all x1, waiting for transfers between devices, by_rows(): lax.all_to_all(inverse, 'tensor', 0, 1, axis_index_groups=across, tiled=T...  34.8 us
    dot_general x1, matrix products, by_rows(): jnp.einsum('nokb,kbc->nokc', query.reshape(number, wide, blocks, size), b...  25.4 us
    gather x1, local copies, waits for them, and re-layouts, pick_scores(): return jnp.take_along_axis(picked, token_ids, axis=1)  24.7 us
    all_gather x1, waiting for transfers between devices, by_rows(): lax.all_gather(act, 'tensor', axis=0, axis_index_groups=across, tiled=True)  21.4 us
    all_to_all x1, blocking collectives, by_rows(): lax.all_to_all(query, 'tensor', 3, 1, axis_index_groups=pairs, tiled=True)  18.5 us
    reshape x1, local copies, waits for them, and re-layouts, by_rows(): query = query_grads.reshape(number, rows, chips, 2, width)  14.7 us
    reshape x1, local copies, waits for them, and re-layouts, by_rows(): query.reshape(number, wide, blocks, size)  14 us
  transfers between devices with their start and end apart: 5, of which 3 were waited for; matrix products, arithmetic and copies ran while one was open for 33% of the time, Pallas kernels for 0%

profile of v1, /device:TPU:0, one launch (start us, length us, event | category | flops | bytes accessed | tf_op | source)
XLA Modules:
  0.0 326.0 jit_solution(16726700547131074502)
XLA Ops:
  6.5 0.7 all-gather.3.cloned.1.call-update
  7.3 1.8 copy.55
  9.0 3.4 %all-to-all-start.2 = ((bf16[8,16,2,512]{3,1,0,2:T(8,128)(2,1)}), bf16[8,16,2,512]{3,1,0,2:T(8,128)(2,1)S(1)}, u32[]{:S(2)}, u32[]{:S(2)}) async-start(bf16[8,16,2,512]{3,1,0,2:T(8,128)(2,1)} %copy.55), calls=%async_computation.2 | async-start | bytes 524288 | tf_op jit(solution)/shard_map/all_to_all | solution.py:106
  12.5 12.0 %copy.48 = bf16[2,128,16384]{1,2,0:T(8,128)(2,1)} copy(bf16[2,128,16384]{2,1,0:T(8,128)(2,1)} %param.9) | data formatting | bytes 16777216 | tf_op args[0]
  24.5 14.7 %copy.49 = bf16[2,128,16,2,512]{4,2,1,0,3:T(8,128)(2,1)} copy(bf16[2,128,16,2,512]{1,4,3,2,0:T(8,128)(2,1)} %bitcast.81) | data formatting | bytes 16777216 | tf_op jit(solution)/shard_map/reshape | solution.py:109
  39.1 18.5 %all_to_all.59 = bf16[2,128,16,2,512]{4,2,1,0,3:T(8,128)(2,1)} all-to-all(bf16[2,128,16,2,512]{4,2,1,0,3:T(8,128)(2,1)} %copy.49), channel_id=1, replica_groups={{0,1},{2,3},{4,5},{6,7},{8,9},{10,11},{12,13},{14,15},{16,17},{18,19},{..., dimensions={3} | all-to-all | bytes 16777216 | tf_op jit(solution)/shard_map/all_to_all | solution.py:110
  57.7 8.3 %all-to-all-start.3 = ((bf16[8,16,256]{2,0,1:T(8,128)(2,1)}), bf16[8,16,256]{2,0,1:T(8,128)(2,1)S(1)}, u32[]{:S(2)}, u32[]{:S(2)}) async-start(bf16[8,16,256]{2,0,1:T(8,128)(2,1)} %bitcast.20), calls=%async_computation.3 | async-start | bytes 131072 | tf_op jit(solution)/shard_map/all_to_all | solution.py:112
  66.0 6.6 %divide_convert_fusion = bf16[4096,512]{1,0:T(8,128)(2,1)} fusion(f32[4096,512]{1,0:T(8,128)} %param.10), kind=kLoop, calls=%fused_computation.8 | loop fusion | flops 6291456 | bytes 12582912 | tf_op jit(solution)/shard_map/convert_element_type | solution.py:102
  72.6 1.3 all-to-all-done.3
  73.9 5.6 %all-to-all-start.1 = ((bf16[16,256,512]{2,1,0:T(8,128)(2,1)}), bf16[16,256,512]{2,1,0:T(8,128)(2,1)}, u32[]{:S(2)}, u32[]{:S(2)}) async-start(bf16[16,256,512]{2,1,0:T(8,128)(2,1)} %bitcast.82), calls=%async_computation.1 | async-start | bytes 8388608 | tf_op jit(solution)/shard_map/all_to_all | solution.py:103
  79.6 0.9 copy.71
  80.5 7.7 %copy.50 = bf16[2,2,128,16,1,512]{5,3,2,1,0,4:T(8,128)(2,1)} copy(bf16[2,2,128,16,1,512]{5,3,2,0,1,4:T(8,128)(2,1)} %bitcast.80) | data formatting | bytes 16777216 | tf_op jit(solution)/shard_map/all_to_all | solution.py:110
  88.2 14.0 %reshape.111 = bf16[2,256,64,128]{3,2,1,0:T(8,128)(2,1)} reshape(bf16[2,2,128,16,1,512]{5,3,2,1,0,4:T(8,128)(2,1)} %copy.50) | data formatting | bytes 16777216 | tf_op jit(solution)/shard_map/reshape | solution.py:121
  102.2 0.6 gather_fusion
  102.8 1.9 all_gather.16
  104.7 0.1 fusion.16
  104.8 2.1 all_gather.19
  106.9 0.2 fusion.10
  107.1 0.1 copy.62
  107.3 25.4 %convert_bitcast_fusion.1 = bf16[2,256,64,128]{1,3,0,2:T(8,128)(2,1)} fusion(bf16[2,256,64,128]{3,2,1,0:T(8,128)(2,1)} %reshape.111, bf16[64,128,128]{2,1,0:T(8,128)(2,1)} %all-gather.3.cloned.1.call-done), kind=kOutput, calls=%fused_computation.9 | convolution fusion | flops 1077936128 | bytes 18874368 | tf_op jit(solution)/shard_map/nokb,kbc->nokc/dot_general | solution.py:120
  132.6 7.8 %copy.53 = bf16[2,256,64,128]{1,3,2,0:T(8,128)(2,1)} copy(bf16[2,256,64,128]{1,3,0,2:T(8,128)(2,1)} %convert_bitcast_fusion.1) | data formatting | bytes 16777216 | tf_op jit(solution)/shard_map/convert_element_type | solution.py:123
  140.5 34.8 %all-to-all-done.1 = bf16[16,256,512]{2,1,0:T(8,128)(2,1)} async-done(((bf16[16,256,512]{2,1,0:T(8,128)(2,1)}), bf16[16,256,512]{2,1,0:T(8,128)(2,1)}, u32[]{:S(2)}, u32[]{:S(2)}) %all-to-all-start.1) | async-done | bytes 4194336 | tf_op jit(solution)/shard_map/all_to_all | solution.py:103
  175.3 6.7 %convert_bitcast_fusion = f32[256,16,512]{2,0,1:T(8,128)} fusion(bf16[16,256,512]{2,1,0:T(8,128)(2,1)} %all-to-all-done.1), kind=kLoop, calls=%fused_computation.7 | loop fusion | flops 2097152 | bytes 12582912 | tf_op jit(solution)/shard_map/convert_element_type | solution.py:125
  182.0 9.3 %copy.54 = f32[256,16,512]{0,2,1:T(8,128)} copy(f32[256,16,512]{2,0,1:T(8,128)} %convert_bitcast_fusion) | data formatting | bytes 16777216 | tf_op jit(solution)/shard_map/convert_element_type | solution.py:125
  191.3 21.4 %all-gather.5.cloned.1.call-done = bf16[256,8192]{1,0:T(8,128)(2,1)} async-done(((bf16[16,8192]{1,0:T(8,128)(2,1)}), bf16[256,8192]{1,0:T(8,128)(2,1)}) %all-gather.5.cloned.1.call-update) | async-done | bytes 4194320 | tf_op jit(solution)/shard_map/all_gather | solution.py:108
  212.6 6.5 %copy.56 = bf16[256,8192]{0,1:T(8,128)(2,1)} copy(bf16[256,8192]{1,0:T(8,128)(2,1)} %all-gather.5.cloned.1.call-done) | data formatting | bytes 8388608 | tf_op jit(solution)/shard_map/all_gather | solution.py:108
  219.1 5.4 %convolution_convert_fusion = bf16[64,128,256]{2,1,0:T(8,128)(2,1)} fusion(bf16[64,128,128]{2,1,0:T(8,128)(2,1)S(1)} %copy-done.2, bf16[256,64,128]{0,2,1:T(8,128)(2,1)} %bitcast.83), kind=kOutput, calls=%fused_computation.11 | convolution fusion | flops 538968064 | bytes 10485760 | tf_op jit(solution)/shard_map/tkb,kbc->tkc/dot_general | solution.py:118
  224.5 13.9 %fusion.9 = f32[2,256]{1,0:T(2,128)S(1)} fusion(bf16[256,8192,1]{0,1,2:T(8,128)(2,1)} %bitcast.86, bf16[2,256,8192]{1,2,0:T(8,128)(2,1)} %bitcast.84, f32[256,8192]{0,1:T(8,128)} %bitcast.85, f32[256,256]{0,1:T(8,128)S(1)} %copy.62, bf16[256,256]{1,0:T(8,128)(2,1)S(1)} %all_gather.16), kind=kOutput, calls=%fused_computation.15 | convolution fusion | flops 4303617536 | bytes 21366784 | tf_op jit(solution)/shard_map/tf,nhf->nth/dot_general | solution.py:126
  238.4 54.7 %psum.7 = f32[2,256]{1,0:T(2,128)S(1)} all-reduce(f32[2,256]{1,0:T(2,128)S(1)} %fusion.9), channel_id=1, replica_groups=mesh['groups'=1,'tensor'=32] {'tensor'}, use_global_device_ids=true, to_apply=%region_1.0 | all-reduce | flops 512 | bytes 4096 | tf_op jit(solution)/shard_map/psum | solution.py:128
  293.1 0.6 gather_fusion.1
  293.7 24.7 %gather_fusion.2 = f32[3072]{0:T(1024)S(1)} fusion(f32[24,256]{1,0:T(8,128)S(1)} %broadcast_select_fusion, s32[3072]{0:T(1024)S(1)} %fusion.16), kind=kCustom, calls=%fused_computation.2 | custom fusion | bytes 49152 | tf_op jit(solution)/shard_map/jit(take_along_axis)/gather | solution.py:25
  318.4 0.7 bitcast_select_fusion
  (25 shorter events, 0.2 us)
Async XLA Ops:
  6.5 95.7 %copy-start = (s32[256]{0:T(256)S(1)}, s32[256]{0:T(256)}, u32[]{:S(2)}) copy-start(s32[256]{0:T(256)} %param.15) | copy-start | bytes 3076
  6.5 100.7 %all-gather.3.cloned.1.call-start = ((), (), s32[]{:S(2)}) async-start(), calls=%async_computation.4 | async-start | bytes 2228224 | tf_op jit(solution)/shard_map/all_gather | solution.py:104
  9.0 30.1 %all-to-all-start.2 = ((bf16[8,16,2,512]{3,1,0,2:T(8,128)(2,1)}), bf16[8,16,2,512]{3,1,0,2:T(8,128)(2,1)S(1)}, u32[]{:S(2)}, u32[]{:S(2)}) async-start(bf16[8,16,2,512]{3,1,0,2:T(8,128)(2,1)} %copy.55), calls=%async_computation.2 | async-start | bytes 524288 | tf_op jit(solution)/shard_map/all_to_all | solution.py:106
  57.7 16.3 %all-to-all-start.3 = ((bf16[8,16,256]{2,0,1:T(8,128)(2,1)}), bf16[8,16,256]{2,0,1:T(8,128)(2,1)S(1)}, u32[]{:S(2)}, u32[]{:S(2)}) async-start(bf16[8,16,256]{2,0,1:T(8,128)(2,1)} %bitcast.20), calls=%async_computation.3 | async-start | bytes 131072 | tf_op jit(solution)/shard_map/all_to_all | solution.py:112
  73.9 101.4 %all-to-all-start.1 = ((bf16[16,256,512]{2,1,0:T(8,128)(2,1)}), bf16[16,256,512]{2,1,0:T(8,128)(2,1)}, u32[]{:S(2)}, u32[]{:S(2)}) async-start(bf16[16,256,512]{2,1,0:T(8,128)(2,1)} %bitcast.82), calls=%async_computation.1 | async-start | bytes 8388608 | tf_op jit(solution)/shard_map/all_to_all | solution.py:103
  79.5 133.1 %all-gather.5.cloned.1.call-start = ((), (), s32[]{:S(2)}) async-start(), calls=%async_computation.5 | async-start | bytes 4456448 | tf_op jit(solution)/shard_map/all_gather | solution.py:108
  88.2 14.0 %copy-start.5 = (s32[24]{0:T(128)S(1)}, s32[24]{0:T(128)}, u32[]{:S(2)}) copy-start(s32[24]{0:T(128)} %param.17) | copy-start | bytes 292
  88.2 14.6 %copy-start.3 = (bf16[128,256]{1,0:T(8,128)(2,1)S(1)}, bf16[128,256]{1,0:T(8,128)(2,1)}, u32[]{:S(2)}) copy-start(bf16[128,256]{1,0:T(8,128)(2,1)} %param.12) | copy-start | bytes 196612
  88.2 16.5 %copy-start.4 = (s32[24]{0:T(128)S(1)}, s32[24]{0:T(128)}, u32[]{:S(2)}) copy-start(s32[24]{0:T(128)} %param.16) | copy-start | bytes 292
  191.3 27.8 %copy-start.2 = (bf16[64,128,128]{2,1,0:T(8,128)(2,1)S(1)}, bf16[64,128,128]{2,1,0:T(8,128)(2,1)}, u32[]{:S(2)}) copy-start(bf16[64,128,128]{2,1,0:T(8,128)(2,1)} %all-gather.3.cloned.1.call-done) | copy-start | bytes 6291460
  224.5 94.6 %copy-start.1 = (s32[256]{0:T(256)S(1)}, s32[256]{0:T(256)}, u32[]{:S(2)}) copy-start(s32[256]{0:T(256)} %param.15) | copy-start | bytes 3076
Sparse Core Ops, SparseCore 0:
  10.1 65.1 all-gather.2
  83.2 129.4 all-gather.4

commit v2 on v1

--- a/solution.py
+++ b/solution.py
@@ -1,6 +1,8 @@
 import jax
 import jax.numpy as jnp
 from jax import lax
+from jax.experimental import pallas as pl
+from jax.experimental.pallas import tpu as pltpu
 from jax.sharding import PartitionSpec as P
 
 BLOCK = 128
@@ -76,6 +78,382 @@
     return lax.psum(pick_scores(totals, block_tokens, pair_query, pair_block), "tensor")
 
 
+CHIPS = 16
+PLANE = 4
+
+
+def fused_kernel(
+    query_hbm,
+    eigen_hbm,
+    basis_hbm,
+    grad_hbm,
+    act_in,
+    cot_in,
+    out_ref,
+    eigen,
+    inverse_out,
+    inverse_in,
+    query,
+    rotated,
+    act,
+    basis,
+    grad,
+    act_pair,
+    cot_mine,
+    cot_pair,
+    cot,
+    sums,
+    pair_sums,
+    all_sums,
+    eigen_sem,
+    local_sem,
+    query_local,
+    query_send,
+    query_recv,
+    pair_send,
+    pair_recv,
+    inverse_send,
+    inverse_recv,
+    act_send,
+    act_recv,
+    basis_send,
+    basis_recv,
+    cot_send,
+    cot_recv,
+    sums_send,
+    sums_recv,
+):
+    bf16, f32 = jnp.bfloat16, jnp.float32
+    me = lax.axis_index("tensor")
+    core = lax.rem(me, 2)
+    chip = me // 2
+    z = chip // PLANE
+    y = lax.rem(chip // 2, 2)
+    x = lax.rem(chip, 2)
+    number, rows = query_hbm.shape[0], query_hbm.shape[1]
+    width = eigen_hbm.shape[1]
+    wide = 2 * rows
+    half = CHIPS * width
+    tokens = act_in.shape[1]
+    both = 2 * tokens
+    size = basis_hbm.shape[1]
+
+    def device(at_chip, at_core):
+        return {"tensor": 2 * at_chip + at_core}
+
+    def remote(src, dst, send, recv, to):
+        return pltpu.make_async_remote_copy(
+            src_ref=src,
+            dst_ref=dst,
+            send_sem=send,
+            recv_sem=recv,
+            device_id=to,
+            device_id_type=pl.DeviceIdType.MESH,
+        )
+
+    other = device(chip, 1 - core)
+
+    def nth(step):
+        return lax.rem(chip + step, CHIPS)
+
+    def eigen_load(c):
+        return pltpu.make_async_copy(eigen_hbm.at[pl.ds(c * wide, wide), :], eigen.at[c], eigen_sem.at[c])
+
+    def query_load(c):
+        columns = pl.ds(pl.multiple_of((2 * c + core) * width, width), width)
+        mine = pl.ds(pl.multiple_of(core * rows, rows), rows)
+        return pltpu.make_async_copy(query_hbm.at[:, :, columns], query.at[c, :, mine, :], query_local.at[c])
+
+    def query_pass(c):
+        columns = pl.ds(pl.multiple_of((2 * c + 1 - core) * width, width), width)
+        mine = pl.ds(pl.multiple_of(core * rows, rows), rows)
+        return remote(query_hbm.at[:, :, columns], query.at[c, :, mine, :], query_send.at[c], query_recv.at[c], other)
+
+    @pl.loop(0, CHIPS)
+    def _(step):
+        eigen_load(nth(step)).start()
+
+    grad_rows = pl.ds(pl.multiple_of(core * rows, rows), rows)
+    grad_load = pltpu.make_async_copy(grad_hbm, grad.at[grad_rows, :], local_sem.at[0])
+    grad_load.start()
+    basis_load = pltpu.make_async_copy(basis_hbm, basis.at[chip], local_sem.at[1])
+    basis_load.start()
+
+    barrier = pltpu.get_barrier_semaphore()
+    pl.semaphore_signal(barrier, inc=1, device_id=other, device_id_type=pl.DeviceIdType.MESH)
+
+    @pl.loop(1, CHIPS)
+    def _(step):
+        pl.semaphore_signal(
+            barrier, inc=1, device_id=device(nth(step), core), device_id_type=pl.DeviceIdType.MESH
+        )
+
+    pl.semaphore_wait(barrier, CHIPS)
+
+    act_pass = remote(act_in.at[1 - core], act_pair, pair_send.at[0], pair_recv.at[0], other)
+    cot_pass = remote(cot_in, cot_pair, pair_send.at[1], pair_recv.at[1], other)
+    grad_pass = remote(grad_hbm, grad.at[grad_rows, :], pair_send.at[2], pair_recv.at[2], other)
+    act_pass.start()
+    cot_pass.start()
+    grad_pass.start()
+
+    x_to = device(z * PLANE + y * 2 + 1 - x, core)
+    y_to = device(z * PLANE + (1 - y) * 2 + x, core)
+
+    def act_rows(c):
+        return act.at[pl.ds(pl.multiple_of(c * both, both), both), :]
+
+    def act_copy(c, way, to):
+        return remote(act_rows(c), act_rows(c), act_send.at[way, c], act_recv.at[c], to)
+
+    def basis_copy(c, way, to):
+        return remote(basis.at[c], basis.at[c], basis_send.at[way, c], basis_recv.at[c], to)
+
+    def spread(copy, c):
+        copy(c, 0, x_to).start()
+        copy(c, 1, y_to).start()
+
+    def up(copy, c):
+        @pl.when(z < CHIPS // PLANE - 1)
+        def _():
+            copy(c, 2, device(chip + PLANE, core)).start()
+
+    def down(copy, c):
+        @pl.when(z > 0)
+        def _():
+            copy(c, 3, device(chip - PLANE, core)).start()
+
+    basis_load.wait()
+    up(basis_copy, chip)
+    down(basis_copy, chip)
+
+    act_pass.wait_recv()
+
+    def join(first, second):
+        return jnp.concatenate([first, second], axis=0).astype(bf16)
+
+    @pl.when(core == 0)
+    def _():
+        act_rows(chip)[...] = join(act_in[0], act_pair[...])
+
+    @pl.when(core == 1)
+    def _():
+        act_rows(chip)[...] = join(act_pair[...], act_in[1])
+
+    up(act_copy, chip)
+    down(act_copy, chip)
+    spread(basis_copy, chip)
+    spread(act_copy, chip)
+
+    def inverse_copy(c):
+        return remote(
+            inverse_out.at[c], inverse_in.at[chip], inverse_send.at[c], inverse_recv.at[chip], device(c, core)
+        )
+
+    def inverse_arrival(c):
+        return remote(inverse_out.at[c], inverse_in.at[c], inverse_send.at[c], inverse_recv.at[c], other)
+
+    @pl.loop(1, CHIPS)
+    def _(step):
+        c = nth(step)
+        eigen_load(c).wait()
+        inverse_out[c] = (1.0 / (eigen[c] + damping)).astype(bf16)
+        inverse_copy(c).start()
+
+    @pl.loop(0, CHIPS)
+    def _(step):
+        query_load(nth(step)).start()
+        query_pass(nth(step)).start()
+
+    eigen_load(chip).wait()
+    inverse_in[chip] = (1.0 / (eigen[chip] + damping)).astype(bf16)
+
+    cot_pass.wait_recv()
+
+    @pl.when(core == 0)
+    def _():
+        cot_mine[...] = join(cot_in[...], cot_pair[...])
+
+    @pl.when(core == 1)
+    def _():
+        cot_mine[...] = join(cot_pair[...], cot_in[...])
+
+    def cot_columns(c):
+        return cot_mine.at[:, pl.ds(pl.multiple_of(c * wide, wide), wide)]
+
+    def cot_rows(c):
+        return cot.at[pl.ds(pl.multiple_of(c * both, both), both), :]
+
+    def cot_copy(c):
+        return remote(cot_columns(c), cot_rows(chip), cot_send.at[c], cot_recv.at[chip], device(c, core))
+
+    def cot_arrival(c):
+        return remote(cot_columns(c), cot_rows(c), cot_send.at[c], cot_recv.at[c], other)
+
+    @pl.loop(1, CHIPS)
+    def _(step):
+        cot_copy(nth(step)).start()
+
+    cot_rows(chip)[...] = cot_columns(chip)[...]
+
+    levels = CHIPS // PLANE
+    for step in range(1, levels):
+        @pl.when(z >= step)
+        def _():
+            c = chip - step * PLANE
+            for copy in (basis_copy, act_copy):
+                copy(c, 0, x_to).wait_recv()
+                up(copy, c)
+                spread(copy, c)
+
+        @pl.when(z + step < levels)
+        def _():
+            c = chip + step * PLANE
+            for copy in (basis_copy, act_copy):
+                copy(c, 0, x_to).wait_recv()
+                down(copy, c)
+                spread(copy, c)
+
+    def level(step):
+        return lax.rem(z + step, levels) * PLANE
+
+    def at_x(step):
+        return level(step) + y * 2 + 1 - x
+
+    def at_y(step):
+        return level(step) + (1 - y) * 2 + x
+
+    def at_both(step):
+        return level(step) + (1 - y) * 2 + 1 - x
+
+    @pl.loop(0, levels)
+    def _(step):
+        basis_copy(at_x(step), 0, x_to).wait_recv()
+        act_copy(at_x(step), 0, x_to).wait_recv()
+        act_copy(at_x(step), 1, y_to).start()
+        act_copy(at_y(step), 0, x_to).wait_recv()
+        basis_copy(at_y(step), 0, x_to).wait_recv()
+        basis_copy(at_y(step), 0, x_to).start()
+
+    grad_load.wait()
+    grad_pass.wait_recv()
+
+    def turn(values, c):
+        parts = [
+            jnp.dot(
+                values[:, k * size:(k + 1) * size],
+                basis[c, k * size:(k + 1) * size, :],
+                preferred_element_type=f32,
+            )
+            for k in range(width // size)
+        ]
+        return jnp.concatenate(parts, axis=1).astype(bf16)
+
+    def rotate(c):
+        query_load(c).wait()
+        query_pass(c).wait_recv()
+        for q in range(number):
+            rotated[c, q] = lax.dot_general(
+                grad[...], turn(query[c, q], c), (((0,), (0,)), ((), ())), preferred_element_type=f32
+            )
+
+    @pl.loop(0, levels)
+    def _(step):
+        rotate(level(step) + y * 2 + x)
+        rotate(at_x(step))
+        rotate(at_y(step))
+
+    @pl.loop(0, levels)
+    def _(step):
+        basis_copy(at_both(step), 0, x_to).wait_recv()
+        rotate(at_both(step))
+        act_copy(at_both(step), 0, x_to).wait_recv()
+
+    sums[...] = jnp.zeros_like(sums)
+
+    def score(c):
+        columns = pl.ds(pl.multiple_of(c * width, width), width)
+        act_rot = turn(act[:, columns], c)
+        scale = inverse_in[c].astype(f32)
+        for q in range(number):
+            precond = (rotated[c, q] * scale).astype(bf16)
+            sums[q] += lax.dot_general(precond, act_rot, (((1,), (1,)), ((), ())), preferred_element_type=f32)
+
+    score(chip)
+
+    @pl.loop(1, CHIPS)
+    def _(step):
+        c = lax.rem(chip + CHIPS - step, CHIPS)
+        inverse_arrival(c).wait_recv()
+        score(c)
+
+    @pl.loop(1, CHIPS)
+    def _(step):
+        cot_arrival(nth(step)).wait_recv()
+
+    cot_rot = lax.dot_general(grad[...], cot[...], (((0,), (1,)), ((), ())), preferred_element_type=f32)
+    cot_rot = cot_rot.astype(bf16).astype(f32)
+    for q in range(number):
+        pair_sums[core, q:q + 1, :] = jnp.sum(sums[q] * cot_rot, axis=0, keepdims=True)
+
+    core_copy = remote(pair_sums.at[core], pair_sums.at[core], pair_send.at[3], pair_recv.at[3], other)
+    core_copy.start()
+    core_copy.wait()
+    all_sums[chip] = pair_sums[0] + pair_sums[1]
+
+    def sums_copy(c):
+        return remote(all_sums.at[chip], all_sums.at[chip], sums_send.at[c], sums_recv.at[chip], device(c, core))
+
+    def sums_arrival(c):
+        return remote(all_sums.at[c], all_sums.at[c], sums_send.at[c], sums_recv.at[c], other)
+
+    @pl.loop(1, CHIPS)
+    def _(step):
+        sums_copy(nth(step)).start()
+
+    act_pass.wait_send()
+    cot_pass.wait_send()
+    grad_pass.wait_send()
+
+    @pl.loop(0, CHIPS)
+    def _(step):
+        query_pass(nth(step)).wait_send()
+
+    @pl.loop(1, CHIPS)
+    def _(step):
+        inverse_copy(nth(step)).wait_send()
+        cot_copy(nth(step)).wait_send()
+
+    for copy in (basis_copy, act_copy):
+        for step in range(levels):
+            c = level(step) + y * 2 + x
+            copy(c, 0, x_to).wait_send()
+            copy(c, 1, y_to).wait_send()
+        for step in range(levels):
+            @pl.when((z >= step) & (z < levels - 1))
+            def _():
+                copy(chip - step * PLANE, 2, x_to).wait_send()
+
+            @pl.when((z + step < levels) & (z > 0))
+            def _():
+                copy(chip + step * PLANE, 3, x_to).wait_send()
+
+    @pl.loop(0, levels)
+    def _(step):
+        act_copy(at_x(step), 1, y_to).wait_send()
+        basis_copy(at_y(step), 0, x_to).wait_send()
+
+    @pl.loop(1, CHIPS)
+    def _(step):
+        sums_arrival(nth(step)).wait_recv()
+
+    @pl.loop(1, CHIPS)
+    def _(step):
+        sums_copy(nth(step)).wait_send()
+
+    out_ref[...] = jnp.sum(all_sums[...], axis=0)
+
+
 def by_rows(
     query_grads,
     eigen_values,
@@ -87,45 +465,68 @@
     pair_query,
     pair_block,
 ):
-    devices = lax.axis_size("tensor")
-    chips = devices // 2
-    across = [[2 * chip + core for chip in range(chips)] for core in range(2)]
-    pairs = [[2 * chip, 2 * chip + 1] for chip in range(chips)]
     bf16, f32 = jnp.bfloat16, jnp.float32
-
     number, rows, hidden = query_grads.shape
-    width = eigen_values.shape[1]
+    features, width = eigen_values.shape
     wide = 2 * rows
     half = hidden // 2
     tokens = activations.shape[0]
-
-    inverse = (1.0 / (eigen_values + damping)).astype(bf16)
-    inverse = lax.all_to_all(inverse, "tensor", 0, 1, axis_index_groups=across, tiled=True)
-    basis = lax.all_gather(act_basis, "tensor", axis=0, axis_index_groups=across, tiled=True)
-    act = activations.reshape(tokens, chips, 2, width)
-    act = lax.all_to_all(act, "tensor", 2, 0, axis_index_groups=pairs, tiled=True)
-    act = act.reshape(2 * tokens, half)
-    act = lax.all_gather(act, "tensor", axis=0, axis_index_groups=across, tiled=True)
-    query = query_grads.reshape(number, rows, chips, 2, width)
-    query = lax.all_to_all(query, "tensor", 3, 1, axis_index_groups=pairs, tiled=True)
-    grad = lax.all_gather(grad_basis, "tensor", axis=0, axis_index_groups=pairs, tiled=True)
-    cot = lax.all_to_all(cotangents, "tensor", 1, 0, axis_index_groups=across, tiled=True)
-    cot = lax.all_gather(cot, "tensor", axis=0, axis_index_groups=pairs)
-    cot = cot.reshape(2, chips, tokens, wide).transpose(1, 0, 2, 3).reshape(devices * tokens, wide)
-
-    cot_rot = jnp.dot(cot, grad, preferred_element_type=f32).astype(bf16)
-    blocks, size, _ = basis.shape
-    act_rot = jnp.einsum("tkb,kbc->tkc", act.reshape(-1, blocks, size), basis, preferred_element_type=f32)
-    act_rot = act_rot.astype(bf16).reshape(-1, half)
-    turned = jnp.einsum(
-        "nokb,kbc->nokc", query.reshape(number, wide, blocks, size), basis, preferred_element_type=f32
+    all_tokens = 2 * CHIPS * tokens
+    blocks, size, _ = act_basis.shape
+
+    act = activations.reshape(tokens, CHIPS, 2, width).transpose(2, 0, 1, 3).reshape(2, tokens, half).astype(f32)
+    cot = cotangents.astype(f32)
+    vmem, dma = pltpu.VMEM, pltpu.SemaphoreType.DMA
+    totals = pl.pallas_call(
+        fused_kernel,
+        out_shape=jax.ShapeDtypeStruct((number, all_tokens), f32),
+        in_specs=[pl.BlockSpec(memory_space=pl.ANY)] * 4 + [pl.BlockSpec(memory_space=pltpu.VMEM)] * 2,
+        out_specs=pl.BlockSpec(memory_space=pltpu.VMEM),
+        scratch_shapes=[
+            vmem((CHIPS, wide, width), f32),
+            vmem((CHIPS, wide, width), bf16),
+            vmem((CHIPS, wide, width), bf16),
+            vmem((CHIPS, number, wide, width), bf16),
+            vmem((CHIPS, number, wide, width), f32),
+            vmem((all_tokens, half), bf16),
+            vmem((CHIPS, blocks * size, size), bf16),
+            vmem((wide, wide), bf16),
+            vmem((tokens, half), f32),
+            vmem((2 * tokens, features), bf16),
+            vmem((tokens, features), f32),
+            vmem((all_tokens, wide), bf16),
+            vmem((number, wide, all_tokens), f32),
+            vmem((2, number, all_tokens), f32),
+            vmem((CHIPS, number, all_tokens), f32),
+            dma((CHIPS,)),
+            dma((2,)),
+            dma((CHIPS,)),
+            dma((CHIPS,)),
+            dma((CHIPS,)),
+            dma((4,)),
+            dma((4,)),
+            dma((CHIPS,)),
+            dma((CHIPS,)),
+            dma((4, CHIPS)),
+            dma((CHIPS,)),
+            dma((4, CHIPS)),
+            dma((CHIPS,)),
+            dma((CHIPS,)),
+            dma((CHIPS,)),
+            dma((CHIPS,)),
+            dma((CHIPS,)),
+        ],
+        compiler_params=pltpu.CompilerParams(
+            collective_id=0, has_side_effects=True, vmem_limit_bytes=60 * 1024 * 1024
+        ),
+        cost_estimate=pl.CostEstimate(flops=7 * 10**9, bytes_accessed=24 * 10**6, transcendentals=0),
+    )(query_grads, eigen_values, act_basis.reshape(blocks * size, size), grad_basis, act, cot)
+    in_order = jnp.where(block_tokens[None, :, None] == jnp.arange(all_tokens)[None, None, :], totals[:, None, :], 0.0)
+    in_order = jnp.sum(in_order, axis=2).reshape(number, -1, BLOCK)
+    listed = (pair_query[:, None, None] == jnp.arange(number)[None, :, None]) & (
+        pair_block[:, None, None] == jnp.arange(in_order.shape[1])[None, None, :]
     )
-    turned = turned.astype(bf16).reshape(number, wide, half)
-    rotated = jnp.einsum("gh,ngf->nhf", grad, turned, preferred_element_type=f32)
-    precond = (rotated * inverse.astype(f32)).astype(bf16)
-    values = jnp.einsum("tf,nhf->nth", act_rot, precond, preferred_element_type=f32)
-    totals = jnp.sum(values * cot_rot.astype(f32), axis=2)
-    return pick_scores(lax.psum(totals, "tensor"), block_tokens, pair_query, pair_block)
+    return jnp.sum(jnp.where(listed[..., None], in_order[None], 0.0), axis=(1, 2))
 
 
 def solution(mesh):
@@ -133,7 +534,7 @@
 
     def per_device(*args):
         query_grads, grad_basis = args[0], args[3]
-        paired = devices % 2 == 0 and 2 * query_grads.shape[1] == grad_basis.shape[1]
+        paired = devices == 2 * CHIPS and 2 * query_grads.shape[1] == grad_basis.shape[1]
         return (by_rows if paired else by_columns)(*args)
 
     return jax.shard_map(

time: 328 us -> 191 us (0.58)
  Pallas kernels: 0 us -> 186 us
  local copies, waits for them, and re-layouts: 101 us -> 1.82 us
  blocking collectives: 77.2 us -> 0 us
  waiting for transfers between devices: 58.3 us -> 0 us
  matrix products: 44.9 us -> 0 us
  starting transfers between devices: 17.3 us -> 0 us
  between operations: 13.5 us -> 0.06 us
  other arithmetic: 14.2 us -> 3.09 us
    pallas_call x0 -> x1, Pallas kernels: none -> 186 us  [by_rows(): pl.pallas_call(fused_kernel, out_shape=jax.ShapeDtypeStruct((number, all_...]
    psum x1 -> x0, blocking collectives: 54.7 us -> none  [by_rows(): lax.psum(totals, 'tensor')]
    dot_general x4 -> x0, matrix products: 44.9 us -> none  [the longest x1 25.4 us: by_rows(): jnp.einsum('nokb,kbc->nokc', query.reshape(number, wide, blocks, size), b...]
    all_to_all x3 -> x0, waiting for transfers between devices: 36.2 us -> none  [the longest x1 34.8 us: by_rows(): lax.all_to_all(inverse, 'tensor', 0, 1, axis_index_groups=across, tiled=T...]
    reshape x3 -> x0, local copies, waits for them, and re-layouts: 30.5 us -> none  [the longest x1 14.7 us: by_rows(): query = query_grads.reshape(number, rows, chips, 2, width)]
    gather x3 -> x0, local copies, waits for them, and re-layouts: 25.9 us -> none  [the longest x1 24.7 us: pick_scores(): return jnp.take_along_axis(picked, token_ids, axis=1)]
    all_gather x2 -> x0, waiting for transfers between devices: 21.4 us -> none  [the longest x1 21.4 us: by_rows(): lax.all_gather(act, 'tensor', axis=0, axis_index_groups=across, tiled=True)]
    all_to_all x1 -> x0, blocking collectives: 18.5 us -> none  [by_rows(): lax.all_to_all(query, 'tensor', 3, 1, axis_index_groups=pairs, tiled=True)]
  transfers between devices with their start and end apart: 5 -> 0, of which waited for: 3 -> 0; matrix products, arithmetic and copies ran while one was open for 33% -> 0% of each run, Pallas kernels for 0% -> 0%
where the time goes in v2:
time: 191 us
  Pallas kernels  186 us (97%)
  other arithmetic  3.09 us (2%)
    pallas_call x1, Pallas kernels, by_rows(): pl.pallas_call(fused_kernel, out_shape=jax.ShapeDtypeStruct((number, all_...  186 us

profile of v2, /device:TPU:0, one launch (start us, length us, event | category | flops | bytes accessed | tf_op | source)
XLA Modules:
  0.0 190.9 jit_solution(5110682049312681164)
XLA Ops:
  0.0 1.8 copy.11
  1.8 1.5 convert_element_type.16.cot_in
  3.3 0.0 copy-start
  3.3 0.0 copy-start.1
  3.3 0.0 copy-start.2
  3.3 185.9 %shard_map.91 = f32[2,256]{1,0:T(2,128)} custom-call(bf16[2,128,16384]{2,1,0:T(8,128)(2,1)} %query_hbm.1, f32[4096,512]{1,0:T(8,128)} %eigen_hbm.1, bf16[512,128]{1,0:T(8,128)(2,1)} %bitcast.8, bf16[128,256]{1,0:T(8,128)(2,1)} %grad_hbm.1, f32[2,8,8192]{2,1,0:T(8,128)} %bitcast.6, f32[8,4096]{1,0:T(8,128)} %convert_element_type.16.cot_in), custom_call_target="tpu_custom_call" | custom-call | flops 7000000000 | bytes 24000000 | tf_op jit(solution)/shard_map/pallas_call | solution.py:480
  189.2 0.0 copy-done
  189.2 0.1 iota_compare_fusion
  189.3 0.8 select_reduce_fusion
  190.1 0.0 copy-done.1
  190.1 0.0 copy-done.2
  190.2 0.7 select_reduce_fusion.1
  (3 shorter events, 0.0 us)
Async XLA Ops:
  3.3 185.9 %copy-start = (s32[256]{0:T(256)S(1)}, s32[256]{0:T(256)}, u32[]{:S(2)}) copy-start(s32[256]{0:T(256)} %param.15) | copy-start | bytes 3076
  3.3 186.8 %copy-start.1 = (s32[24]{0:T(128)S(1)}, s32[24]{0:T(128)}, u32[]{:S(2)}) copy-start(s32[24]{0:T(128)} %param.17) | copy-start | bytes 292
  3.3 186.8 %copy-start.2 = (s32[24]{0:T(128)S(1)}, s32[24]{0:T(128)}, u32[]{:S(2)}) copy-start(s32[24]{0:T(128)} %param.16) | copy-start | bytes 292

commit v3 on v0

--- a/solution.py
+++ b/solution.py
@@ -1,6 +1,8 @@
 import jax
 import jax.numpy as jnp
 from jax import lax
+from jax.experimental import pallas as pl
+from jax.experimental.pallas import tpu as pltpu
 from jax.sharding import PartitionSpec as P
 
 BLOCK = 128
@@ -18,7 +20,14 @@
     return turned.astype(jnp.bfloat16).reshape(row_count, nblocks * block_width)
 
 
-def per_device(
+def pick_scores(totals, block_tokens, pair_query, pair_block):
+    blocks = block_tokens.reshape(-1, BLOCK)
+    picked = jnp.take(totals, pair_query, axis=0)
+    token_ids = jnp.take(blocks, pair_block, axis=0)
+    return jnp.take_along_axis(picked, token_ids, axis=1)
+
+
+def by_columns(
     query_grads,
     eigen_values,
     act_basis,
@@ -59,7 +68,6 @@
     rotated = jnp.einsum("cgh,ncgf->nchf", grad_blocks, turned, preferred_element_type=jnp.float32)
     rotated = rotated.reshape(number, model_cols, slice_cols)
     precond = (rotated / (eigen_values + damping)).astype(jnp.bfloat16)
-    blocks = block_tokens.reshape(-1, BLOCK)
     act_wide = act_rot.astype(jnp.float32)
 
     def score_query(matrix):
@@ -67,13 +75,504 @@
         return jnp.sum(values * act_wide, axis=1)
 
     totals = lax.map(score_query, precond)
-    picked = jnp.take(totals, pair_query, axis=0)
-    token_ids = jnp.take(blocks, pair_block, axis=0)
-    partial_value = jnp.take_along_axis(picked, token_ids, axis=1)
-    return lax.psum(partial_value, "tensor")
+    return lax.psum(pick_scores(totals, block_tokens, pair_query, pair_block), "tensor")
+
+
+PLANES = 4
+PLANE = 8
+CHIPS = PLANES * PLANE // 2
+
+
+def fused_kernel(
+    query_hbm,
+    eigen_hbm,
+    basis_hbm,
+    grad_hbm,
+    act_in,
+    cot_in,
+    out_ref,
+    eigen,
+    inverse_out,
+    inverse_in,
+    query,
+    rotated,
+    act_plane,
+    act,
+    act_rot,
+    basis,
+    grad,
+    cot_line,
+    cot,
+    sums,
+    plane_sums,
+    line_sums,
+    eigen_sem,
+    local_sem,
+    query_local,
+    query_send,
+    query_recv,
+    inverse_send,
+    inverse_recv,
+    plane_send,
+    plane_recv,
+    act_send,
+    act_recv,
+    basis_send,
+    basis_recv,
+    line_send,
+    line_recv,
+):
+    bf16, f32 = jnp.bfloat16, jnp.float32
+    me = lax.axis_index("tensor")
+    z = me // PLANE
+    place = lax.rem(me, PLANE)
+    number, rows = query_hbm.shape[0], query_hbm.shape[1]
+    width = eigen_hbm.shape[1]
+    wide = 2 * rows
+    blocks = PLANE // 2
+    tokens = act_in.shape[1]
+    flock = PLANE * tokens
+    size = basis_hbm.shape[1]
+
+    def remote(src, dst, send, recv, to):
+        return pltpu.make_async_remote_copy(
+            src_ref=src,
+            dst_ref=dst,
+            send_sem=send,
+            recv_sem=recv,
+            device_id={"tensor": to},
+            device_id_type=pl.DeviceIdType.MESH,
+        )
+
+    def in_plane(step):
+        return lax.rem(place + step, PLANE)
+
+    def in_line(step):
+        return lax.rem(z + step, PLANES)
+
+    def at_place(p):
+        return z * PLANE + p
+
+    def at_level(level):
+        return level * PLANE + place
+
+    a_plane = at_place(in_plane(1))
+    a_line = at_level(in_line(1))
+
+    def eigen_load(c):
+        return pltpu.make_async_copy(eigen_hbm.at[pl.ds(c * wide, wide), :], eigen.at[c], eigen_sem.at[c])
+
+    def mine(of):
+        return pl.ds(pl.multiple_of(of * rows, rows), rows)
+
+    def query_columns(j, p):
+        return query_hbm.at[:, :, pl.ds(pl.multiple_of((j * PLANE + p) * width, width), width)]
+
+    def query_load(j):
+        return pltpu.make_async_copy(query_columns(j, place), query.at[j, :, mine(place), :], query_local.at[j])
+
+    def query_copy(j, p):
+        return remote(
+            query_columns(j, p), query.at[j, :, mine(place), :], query_send.at[j, p], query_recv.at[j, place], at_place(p)
+        )
+
+    def query_arrival(j, p):
+        return remote(
+            query_columns(j, p), query.at[j, :, mine(p), :], query_send.at[j, p], query_recv.at[j, p], a_plane
+        )
+
+    @pl.loop(0, PLANES)
+    def _(step):
+        for b in range(blocks):
+            eigen_load(in_line(step + 1) * blocks + b).start()
+
+    grad_load = pltpu.make_async_copy(grad_hbm, grad.at[mine(place), :], local_sem.at[0])
+    grad_load.start()
+    basis_load = pltpu.make_async_copy(basis_hbm, basis.at[z], local_sem.at[1])
+    basis_load.start()
+
+    barrier = pltpu.get_barrier_semaphore()
+    for step in range(1, PLANE):
+        pl.semaphore_signal(
+            barrier, inc=1, device_id={"tensor": at_place(in_plane(step))}, device_id_type=pl.DeviceIdType.MESH
+        )
+    for step in range(1, PLANES):
+        pl.semaphore_signal(
+            barrier, inc=1, device_id={"tensor": at_level(in_line(step))}, device_id_type=pl.DeviceIdType.MESH
+        )
+    pl.semaphore_wait(barrier, PLANE + PLANES - 2)
+
+    def act_copy(p):
+        return remote(act_in.at[p], act_plane.at[place], plane_send.at[0, p], plane_recv.at[0, place], at_place(p))
+
+    def act_arrival(p):
+        return remote(act_in.at[p], act_plane.at[p], plane_send.at[0, p], plane_recv.at[0, p], a_plane)
+
+    def grad_copy(p):
+        return remote(grad_hbm, grad.at[mine(place), :], plane_send.at[1, p], plane_recv.at[1, place], at_place(p))
+
+    def grad_arrival(p):
+        return remote(grad_hbm, grad.at[mine(p), :], plane_send.at[1, p], plane_recv.at[1, p], a_plane)
+
+    def cot_copy(level):
+        return remote(cot_in.at[level], cot_line.at[z], line_send.at[0, level], line_recv.at[0, z], at_level(level))
+
+    def cot_arrival(level):
+        return remote(cot_in.at[level], cot_line.at[level], line_send.at[0, level], line_recv.at[0, level], a_line)
+
+    @pl.loop(1, PLANE)
+    def _(step):
+        act_copy(in_plane(step)).start()
+
+    for step in range(1, PLANES):
+        cot_copy(in_line(step)).start()
+
+    @pl.loop(1, PLANE)
+    def _(step):
+        grad_copy(in_plane(step)).start()
+
+    act_plane[place] = act_in[place]
+    cot_line[z] = cot_in[z]
+
+    def act_rows(level):
+        return act.at[pl.ds(pl.multiple_of(level * flock, flock), flock), :]
+
+    def act_hop(level, way, to):
+        return remote(act_rows(level), act_rows(level), act_send.at[way, level], act_recv.at[level], to)
+
+    def basis_hop(level, way, to):
+        return remote(basis.at[level], basis.at[level], basis_send.at[way, level], basis_recv.at[level], to)
+
+    def up(hop, level):
+        @pl.when(z < PLANES - 1)
+        def _():
+            hop(level, 0, me + PLANE).start()
+
+    def down(hop, level):
+        @pl.when(z > 0)
+        def _():
+            hop(level, 1, me - PLANE).start()
+
+    def pass_on(step):
+        @pl.when(z >= step)
+        def _():
+            for hop in (basis_hop, act_hop):
+                hop(z - step, 0, a_line).wait_recv()
+                up(hop, z - step)
+
+        @pl.when(z + step < PLANES)
+        def _():
+            for hop in (basis_hop, act_hop):
+                hop(z + step, 0, a_line).wait_recv()
+                down(hop, z + step)
+
+    basis_load.wait()
+    up(basis_hop, z)
+    down(basis_hop, z)
+
+    def inverse_copy(level, b):
+        c = level * blocks + b
+        return remote(
+            inverse_out.at[c],
+            inverse_in.at[z * blocks + b],
+            inverse_send.at[c],
+            inverse_recv.at[z * blocks + b],
+            at_level(level),
+        )
+
+    def inverse_arrival(level, b):
+        c = level * blocks + b
+        return remote(inverse_out.at[c], inverse_in.at[c], inverse_send.at[c], inverse_recv.at[c], a_line)
+
+    def invert(step, start, stop):
+        @pl.loop(start, stop)
+        def _(b):
+            c = in_line(step) * blocks + b
+            eigen_load(c).wait()
+            inverse_out[c] = (1.0 / (eigen[c] + damping)).astype(bf16)
+            inverse_copy(in_line(step), b).start()
+
+    def send_query(j):
+        query_load(j).start()
+
+        @pl.loop(1, PLANE)
+        def _(step):
+            query_copy(j, in_plane(step)).start()
+
+    invert(1, 0, 2)
+    send_query(z)
+    invert(1, 2, blocks)
+
+    @pl.loop(1, PLANE)
+    def _(step):
+        act_arrival(in_plane(step)).wait_recv()
+
+    act_rows(z)[...] = jnp.concatenate([act_plane[p] for p in range(PLANE)], axis=0).astype(bf16)
+    up(act_hop, z)
+    down(act_hop, z)
+
+    send_query(in_line(1))
+    invert(2, 0, blocks)
+    send_query(in_line(2))
+
+    def cot_spread(p):
+        return remote(cot.at[place], cot.at[place], plane_send.at[2, p], plane_recv.at[2, place], at_place(p))
+
+    def cot_spread_arrival(p):
+        return remote(cot.at[p], cot.at[p], plane_send.at[2, p], plane_recv.at[2, p], a_plane)
+
+    for step in range(1, PLANES):
+        cot_arrival(in_line(step)).wait_recv()
+    cot[place] = jnp.concatenate([cot_line[level] for level in range(PLANES)], axis=0).astype(bf16)
+
+    @pl.loop(1, PLANE)
+    def _(step):
+        cot_spread(in_plane(step)).start()
+
+    invert(3, 0, blocks)
+    send_query(in_line(3))
+
+    @pl.loop(0, blocks)
+    def _(b):
+        c = z * blocks + b
+        eigen_load(c).wait()
+        inverse_in[c] = (1.0 / (eigen[c] + damping)).astype(bf16)
+
+    grad_load.wait()
+
+    @pl.loop(1, PLANE)
+    def _(step):
+        grad_arrival(in_plane(step)).wait_recv()
+
+    def turn(values, j):
+        parts = [
+            jnp.dot(
+                values[:, k * size:(k + 1) * size],
+                basis[j, k * size:(k + 1) * size, :],
+                preferred_element_type=f32,
+            )
+            for k in range(width // size)
+        ]
+        return jnp.concatenate(parts, axis=1).astype(bf16)
+
+    def grad_block(b):
+        return grad[pl.ds(pl.multiple_of(b * wide, wide), wide), :]
+
+    def rotate(j):
+        query_load(j).wait()
+
+        @pl.loop(1, PLANE)
+        def _(step):
+            query_arrival(j, in_plane(step)).wait_recv()
+
+        @pl.loop(0, blocks)
+        def _(b):
+            these = pl.ds(pl.multiple_of(b * wide, wide), wide)
+            for q in range(number):
+                rotated[j * blocks + b, q] = lax.dot_general(
+                    grad_block(b), turn(query[j, q, these, :], j), (((0,), (0,)), ((), ())), preferred_element_type=f32
+                )
+
+    pass_on(1)
+    rotate(z)
+    pass_on(2)
+    pass_on(3)
+
+    @pl.loop(1, PLANES)
+    def _(step):
+        rotate(in_line(step))
+
+    @pl.loop(0, PLANES)
+    def _(j):
+        act_rot[j] = turn(act[:, pl.ds(pl.multiple_of(j * width, width), width)], j)
+
+    sums[...] = jnp.zeros_like(sums)
+
+    def score(j, b):
+        c = j * blocks + b
+        scale = inverse_in[c].astype(f32)
+        for q in range(number):
+            precond = (rotated[c, q] * scale).astype(bf16)
+            sums[b, q] += lax.dot_general(precond, act_rot[j], (((1,), (1,)), ((), ())), preferred_element_type=f32)
+
+    @pl.loop(0, blocks)
+    def _(b):
+        score(z, b)
+
+    @pl.loop(1, PLANE)
+    def _(step):
+        cot_spread_arrival(in_plane(step)).wait_recv()
+
+    wide_cot = cot[...].astype(f32)
+    pieces = [
+        wide_cot[p, level * tokens:(level + 1) * tokens, :] for level in range(PLANES) for p in range(PLANE)
+    ]
+    cot_rows = jnp.concatenate(pieces, axis=0).astype(bf16)
+
+    @pl.loop(1, PLANES)
+    def _(step):
+        level = lax.rem(z + PLANES - step, PLANES)
+
+        @pl.loop(0, blocks)
+        def _(b):
+            inverse_arrival(level, b).wait_recv()
+            score(level, b)
+
+    totals = [jnp.zeros((1, sums.shape[3]), f32) for _ in range(number)]
+    for b in range(blocks):
+        cot_rot = lax.dot_general(
+            grad[b * wide:(b + 1) * wide, :],
+            cot_rows[:, b * wide:(b + 1) * wide],
+            (((0,), (1,)), ((), ())),
+            preferred_element_type=f32,
+        )
+        cot_rot = cot_rot.astype(bf16).astype(f32)
+        for q in range(number):
+            totals[q] = totals[q] + jnp.sum(sums[b, q] * cot_rot, axis=0, keepdims=True)
+    plane_sums[place] = jnp.concatenate(totals, axis=0)
+
+    def plane_copy(p):
+        return remote(
+            plane_sums.at[place], plane_sums.at[place], plane_send.at[3, p], plane_recv.at[3, place], at_place(p)
+        )
+
+    def plane_arrival(p):
+        return remote(plane_sums.at[p], plane_sums.at[p], plane_send.at[3, p], plane_recv.at[3, p], a_plane)
+
+    def line_copy(level):
+        return remote(line_sums.at[z], line_sums.at[z], line_send.at[1, level], line_recv.at[1, z], at_level(level))
+
+    def line_arrival(level):
+        return remote(line_sums.at[level], line_sums.at[level], line_send.at[1, level], line_recv.at[1, level], a_line)
+
+    @pl.loop(1, PLANE)
+    def _(step):
+        plane_copy(in_plane(step)).start()
+
+    for step in range(1, PLANES):
+        cot_copy(in_line(step)).wait_send()
+        for b in range(blocks):
+            inverse_copy(in_line(step), b).wait_send()
+
+    @pl.loop(1, PLANE)
+    def _(step):
+        p = in_plane(step)
+        act_copy(p).wait_send()
+        grad_copy(p).wait_send()
+        cot_spread(p).wait_send()
+        for j in range(PLANES):
+            query_copy(j, p).wait_send()
+
+    for hop in (basis_hop, act_hop):
+        for step in range(PLANES):
+            @pl.when((z >= step) & (z < PLANES - 1))
+            def _():
+                hop(z - step, 0, a_line).wait_send()
+
+            @pl.when((z + step < PLANES) & (z > 0))
+            def _():
+                hop(z + step, 1, a_line).wait_send()
+
+    @pl.loop(1, PLANE)
+    def _(step):
+        plane_arrival(in_plane(step)).wait_recv()
+
+    line_sums[z] = jnp.sum(plane_sums[...], axis=0)
+    for step in range(1, PLANES):
+        line_copy(in_line(step)).start()
+
+    @pl.loop(1, PLANE)
+    def _(step):
+        plane_copy(in_plane(step)).wait_send()
+
+    for step in range(1, PLANES):
+        line_arrival(in_line(step)).wait_recv()
+    for step in range(1, PLANES):
+        line_copy(in_line(step)).wait_send()
+    out_ref[...] = jnp.sum(line_sums[...], axis=0)
+
+
+def by_rows(
+    query_grads,
+    eigen_values,
+    act_basis,
+    grad_basis,
+    activations,
+    cotangents,
+    block_tokens,
+    pair_query,
+    pair_block,
+):
+    bf16, f32 = jnp.bfloat16, jnp.float32
+    number, rows, hidden = query_grads.shape
+    features, width = eigen_values.shape
+    wide = 2 * rows
+    tokens = activations.shape[0]
+    all_tokens = 2 * CHIPS * tokens
+    blocks, size, _ = act_basis.shape
+
+    split = (tokens, PLANES, PLANE, width)
+    act = activations.reshape(split).transpose(2, 0, 1, 3).reshape(PLANE, tokens, PLANES * width).astype(f32)
+    cot = cotangents.reshape(tokens, PLANES, -1).transpose(1, 0, 2).astype(f32)
+    vmem, dma = pltpu.VMEM, pltpu.SemaphoreType.DMA
+    totals = pl.pallas_call(
+        fused_kernel,
+        out_shape=jax.ShapeDtypeStruct((number, all_tokens), f32),
+        in_specs=[pl.BlockSpec(memory_space=pl.ANY)] * 4 + [pl.BlockSpec(memory_space=pltpu.VMEM)] * 2,
+        out_specs=pl.BlockSpec(memory_space=pltpu.VMEM),
+        scratch_shapes=[
+            vmem((CHIPS, wide, width), f32),
+            vmem((CHIPS, wide, width), bf16),
+            vmem((CHIPS, wide, width), bf16),
+            vmem((PLANES, number, PLANE * rows, width), bf16),
+            vmem((CHIPS, number, wide, width), f32),
+            vmem((PLANE, tokens, PLANES * width), f32),
+            vmem((all_tokens, PLANES * width), bf16),
+            vmem((PLANES, all_tokens, width), bf16),
+            vmem((PLANES, blocks * size, size), bf16),
+            vmem((PLANE * rows, wide), bf16),
+            vmem((PLANES, tokens, features // PLANES), f32),
+            vmem((PLANE, PLANES * tokens, features // PLANES), bf16),
+            vmem((PLANE // 2, number, wide, all_tokens), f32),
+            vmem((PLANE, number, all_tokens), f32),
+            vmem((PLANES, number, all_tokens), f32),
+            dma((CHIPS,)),
+            dma((2,)),
+            dma((PLANES,)),
+            dma((PLANES, PLANE)),
+            dma((PLANES, PLANE)),
+            dma((CHIPS,)),
+            dma((CHIPS,)),
+            dma((4, PLANE)),
+            dma((4, PLANE)),
+            dma((2, PLANES)),
+            dma((PLANES,)),
+            dma((2, PLANES)),
+            dma((PLANES,)),
+            dma((2, PLANES)),
+            dma((2, PLANES)),
+        ],
+        compiler_params=pltpu.CompilerParams(
+            collective_id=0, has_side_effects=True, vmem_limit_bytes=60 * 1024 * 1024
+        ),
+        cost_estimate=pl.CostEstimate(flops=7 * 10**9, bytes_accessed=24 * 10**6, transcendentals=0),
+    )(query_grads, eigen_values, act_basis.reshape(blocks * size, size), grad_basis, act, cot)
+    in_order = jnp.where(block_tokens[None, :, None] == jnp.arange(all_tokens)[None, None, :], totals[:, None, :], 0.0)
+    in_order = jnp.sum(in_order, axis=2).reshape(number, -1, BLOCK)
+    listed = (pair_query[:, None, None] == jnp.arange(number)[None, :, None]) & (
+        pair_block[:, None, None] == jnp.arange(in_order.shape[1])[None, None, :]
+    )
+    return jnp.sum(jnp.where(listed[..., None], in_order[None], 0.0), axis=(1, 2))
 
 
 def solution(mesh):
+    devices = mesh.shape["tensor"]
+
+    def per_device(*args):
+        query_grads, grad_basis = args[0], args[3]
+        paired = devices == 2 * CHIPS and 2 * query_grads.shape[1] == grad_basis.shape[1]
+        return (by_rows if paired else by_columns)(*args)
+
     return jax.shard_map(
         per_device,
         mesh=mesh,

time: 408 us -> 155 us (0.38)
  waiting for transfers between devices: 193 us -> 0 us
  Pallas kernels: 0 us -> 149 us
  local copies, waits for them, and re-layouts: 97 us -> 1.82 us
  blocking collectives: 37 us -> 0 us
  matrix products: 35.4 us -> 0 us
  between operations: 13.6 us -> 0.06 us
  starting transfers between devices: 13.3 us -> 0 us
  other arithmetic: 16.1 us -> 3.09 us
    pallas_call x0 -> x1, Pallas kernels: none -> 149 us  [by_rows(): pl.pallas_call(fused_kernel, out_shape=jax.ShapeDtypeStruct((number, all_...]
    all_to_all x2 -> x0, waiting for transfers between devices: 101 us -> none  [the longest x1 101 us: per_device(): lax.all_to_all(query_grads, 'tensor', split_axis=2, concat_axis=1, tiled=...]
    all_gather x2 -> x0, waiting for transfers between devices: 91.3 us -> none  [the longest x1 91.3 us: per_device(): grad_full = lax.all_gather(grad_basis, 'tensor', axis=0, tiled=True)]
    psum x1 -> x0, blocking collectives: 37 us -> none  [per_device(): return lax.psum(partial_value, 'tensor')]
    dot_general x6 -> x0, matrix products: 35.4 us -> none  [the longest x1 15.2 us: per_device(): jnp.einsum('cgh,ncgf->nchf', grad_blocks, turned, preferred_element_type=...]
    unnamed x16 -> x6, local copies, waits for them, and re-layouts: 31 us -> 0.01 us
    gather x3 -> x0, local copies, waits for them, and re-layouts: 25.9 us -> none  [the longest x1 24.7 us: per_device(): partial_value = jnp.take_along_axis(picked, token_ids, axis=1)]
    reshape x2 -> x0, local copies, waits for them, and re-layouts: 13.4 us -> none  [the longest x1 13.4 us: per_device(): query_piece.reshape(number, model_cols, owned_blocks, act_size)]
  transfers between devices with their start and end apart: 4 -> 0, of which waited for: 2 -> 0; matrix products, arithmetic and copies ran while one was open for 28% -> 0% of each run, Pallas kernels for 0% -> 0%
where the time goes in v3:
time: 155 us; the launch traced here: 154 us
  Pallas kernels  149 us (96%)
  other arithmetic  3.09 us (2%)
  local copies, waits for them, and re-layouts  1.82 us (1%)
    pallas_call x1, Pallas kernels, by_rows(): pl.pallas_call(fused_kernel, out_shape=jax.ShapeDtypeStruct((number, all_...  149 us

profile of v3, /device:TPU:0, one launch (start us, length us, event | category | flops | bytes accessed | tf_op | source)
XLA Modules:
  0.0 154.4 jit_solution(11020912513058102388)
XLA Ops:
  0.0 1.8 %copy.11 = f32[8,4,8,512]{3,0,1,2:T(8,128)} copy(bf16[8,4,8,512]{3,0,2,1:T(8,128)(2,1)} %bitcast.11) | data formatting | bytes 786432 | tf_op jit(solution)/shard_map/convert_element_type | solution.py:515
  1.8 1.5 convert_bitcast_fusion.cot_in
  3.3 0.0 copy-start
  3.3 0.0 copy-start.1
  3.3 0.0 copy-start.2
  3.3 149.4 %shard_map.91 = f32[2,256]{1,0:T(2,128)} custom-call(bf16[2,128,16384]{2,1,0:T(8,128)(2,1)} %query_hbm.1, f32[4096,512]{1,0:T(8,128)} %eigen_hbm.1, bf16[512,128]{1,0:T(8,128)(2,1)} %bitcast.13, bf16[128,256]{1,0:T(8,128)(2,1)} %grad_hbm.1, f32[8,8,2048]{2,1,0:T(8,128)} %bitcast.10, f32[4,8,1024]{2,1,0:T(8,128)} %convert_bitcast_fusion.cot_in), custom_call_target="tpu_custom_call" | custom-call | flops 7000000000 | bytes 24000000 | tf_op jit(solution)/shard_map/pallas_call | solution.py:518
  152.7 0.0 copy-done
  152.7 0.1 iota_compare_fusion
  152.9 0.8 select_reduce_fusion
  153.7 0.0 copy-done.1
  153.7 0.0 copy-done.2
  153.7 0.7 select_reduce_fusion.1
  (3 shorter events, 0.0 us)
Async XLA Ops:
  3.3 149.4 %copy-start = (s32[256]{0:T(256)S(1)}, s32[256]{0:T(256)}, u32[]{:S(2)}) copy-start(s32[256]{0:T(256)} %param.15) | copy-start | bytes 3076
  3.3 150.4 %copy-start.1 = (s32[24]{0:T(128)S(1)}, s32[24]{0:T(128)}, u32[]{:S(2)}) copy-start(s32[24]{0:T(128)} %param.17) | copy-start | bytes 292
  3.3 150.4 %copy-start.2 = (s32[24]{0:T(128)S(1)}, s32[24]{0:T(128)}, u32[]{:S(2)}) copy-start(s32[24]{0:T(128)} %param.16) | copy-start | bytes 292

commit v4 on v3

--- a/solution.py
+++ b/solution.py
@@ -103,6 +103,7 @@
     grad,
     cot_line,
     cot,
+    cot_rot,
     sums,
     plane_sums,
     line_sums,
@@ -299,9 +300,8 @@
         def _(step):
             query_copy(j, in_plane(step)).start()
 
-    invert(1, 0, 2)
+    invert(2, 0, 2)
     send_query(z)
-    invert(1, 2, blocks)
 
     @pl.loop(1, PLANE)
     def _(step):
@@ -311,9 +311,11 @@
     up(act_hop, z)
     down(act_hop, z)
 
-    send_query(in_line(1))
-    invert(2, 0, blocks)
-    send_query(in_line(2))
+    invert(2, 2, blocks)
+    send_query(in_line(PLANES - 2))
+    invert(1, 0, blocks)
+    pass_on(1)
+    send_query(in_line(PLANES - 1))
 
     def cot_spread(p):
         return remote(cot.at[place], cot.at[place], plane_send.at[2, p], plane_recv.at[2, place], at_place(p))
@@ -330,7 +332,8 @@
         cot_spread(in_plane(step)).start()
 
     invert(3, 0, blocks)
-    send_query(in_line(3))
+    send_query(in_line(PLANES - 3))
+    pass_on(2)
 
     @pl.loop(0, blocks)
     def _(b):
@@ -373,19 +376,6 @@
                     grad_block(b), turn(query[j, q, these, :], j), (((0,), (0,)), ((), ())), preferred_element_type=f32
                 )
 
-    pass_on(1)
-    rotate(z)
-    pass_on(2)
-    pass_on(3)
-
-    @pl.loop(1, PLANES)
-    def _(step):
-        rotate(in_line(step))
-
-    @pl.loop(0, PLANES)
-    def _(j):
-        act_rot[j] = turn(act[:, pl.ds(pl.multiple_of(j * width, width), width)], j)
-
     sums[...] = jnp.zeros_like(sums)
 
     def score(j, b):
@@ -395,9 +385,29 @@
             precond = (rotated[c, q] * scale).astype(bf16)
             sums[b, q] += lax.dot_general(precond, act_rot[j], (((1,), (1,)), ((), ())), preferred_element_type=f32)
 
+    rotate(z)
+    pass_on(3)
+
+    @pl.loop(0, PLANES)
+    def _(j):
+        act_rot[j] = turn(act[:, pl.ds(pl.multiple_of(j * width, width), width)], j)
+
     @pl.loop(0, blocks)
     def _(b):
         score(z, b)
+
+    def rotate_and_score(step):
+        level = lax.rem(z + PLANES - step, PLANES)
+        rotate(level)
+
+        @pl.loop(0, blocks)
+        def _(b):
+            inverse_arrival(level, b).wait_recv()
+            score(level, b)
+
+    @pl.loop(1, PLANES - 1)
+    def _(step):
+        rotate_and_score(PLANES - 1 - step)
 
     @pl.loop(1, PLANE)
     def _(step):
@@ -408,27 +418,19 @@
         wide_cot[p, level * tokens:(level + 1) * tokens, :] for level in range(PLANES) for p in range(PLANE)
     ]
     cot_rows = jnp.concatenate(pieces, axis=0).astype(bf16)
-
-    @pl.loop(1, PLANES)
-    def _(step):
-        level = lax.rem(z + PLANES - step, PLANES)
-
-        @pl.loop(0, blocks)
-        def _(b):
-            inverse_arrival(level, b).wait_recv()
-            score(level, b)
-
-    totals = [jnp.zeros((1, sums.shape[3]), f32) for _ in range(number)]
     for b in range(blocks):
-        cot_rot = lax.dot_general(
+        cot_rot[b] = lax.dot_general(
             grad[b * wide:(b + 1) * wide, :],
             cot_rows[:, b * wide:(b + 1) * wide],
             (((0,), (1,)), ((), ())),
             preferred_element_type=f32,
-        )
-        cot_rot = cot_rot.astype(bf16).astype(f32)
+        ).astype(bf16).astype(f32)
+    rotate_and_score(PLANES - 1)
+
+    totals = [jnp.zeros((1, sums.shape[3]), f32) for _ in range(number)]
+    for b in range(blocks):
         for q in range(number):
-            totals[q] = totals[q] + jnp.sum(sums[b, q] * cot_rot, axis=0, keepdims=True)
+            totals[q] = totals[q] + jnp.sum(sums[b, q] * cot_rot[b], axis=0, keepdims=True)
     plane_sums[place] = jnp.concatenate(totals, axis=0)
 
     def plane_copy(p):
@@ -533,6 +535,7 @@
             vmem((PLANE * rows, wide), bf16),
             vmem((PLANES, tokens, features // PLANES), f32),
             vmem((PLANE, PLANES * tokens, features // PLANES), bf16),
+            vmem((PLANE // 2, wide, all_tokens), f32),
             vmem((PLANE // 2, number, wide, all_tokens), f32),
             vmem((PLANE, number, all_tokens), f32),
             vmem((PLANES, number, all_tokens), f32),

time: 155 us -> 155 us (level)
  no operation moved by 1% of the time
where the time goes in v4:
time: 155 us; the launch traced here: 154 us
  Pallas kernels  150 us (97%)
  other arithmetic  3.09 us (2%)
  local copies, waits for them, and re-layouts  1.82 us (1%)
    pallas_call x1, Pallas kernels, by_rows(): pl.pallas_call(fused_kernel, out_shape=jax.ShapeDtypeStruct((number, all_...  150 us

profile of v4, /device:TPU:0, one launch (start us, length us, event | category | flops | bytes accessed | tf_op | source)
XLA Modules:
  0.0 154.5 jit_solution(15693272593726663132)
XLA Ops:
  0.0 1.8 %copy.11 = f32[8,4,8,512]{3,0,1,2:T(8,128)} copy(bf16[8,4,8,512]{3,0,2,1:T(8,128)(2,1)} %bitcast.11) | data formatting | bytes 786432 | tf_op jit(solution)/shard_map/convert_element_type | solution.py:517
  1.8 1.5 convert_bitcast_fusion.cot_in
  3.3 0.0 copy-start
  3.3 0.0 copy-start.1
  3.3 0.0 copy-start.2
  3.3 149.5 %shard_map.91 = f32[2,256]{1,0:T(2,128)} custom-call(bf16[2,128,16384]{2,1,0:T(8,128)(2,1)} %query_hbm.1, f32[4096,512]{1,0:T(8,128)} %eigen_hbm.1, bf16[512,128]{1,0:T(8,128)(2,1)} %bitcast.13, bf16[128,256]{1,0:T(8,128)(2,1)} %grad_hbm.1, f32[8,8,2048]{2,1,0:T(8,128)} %bitcast.10, f32[4,8,1024]{2,1,0:T(8,128)} %convert_bitcast_fusion.cot_in), custom_call_target="tpu_custom_call" | custom-call | flops 7000000000 | bytes 24000000 | tf_op jit(solution)/shard_map/pallas_call | solution.py:520
  152.8 0.0 copy-done
  152.8 0.1 iota_compare_fusion
  153.0 0.8 select_reduce_fusion
  153.8 0.0 copy-done.1
  153.8 0.0 copy-done.2
  153.8 0.7 select_reduce_fusion.1
  (3 shorter events, 0.0 us)
Async XLA Ops:
  3.3 149.5 %copy-start = (s32[256]{0:T(256)S(1)}, s32[256]{0:T(256)}, u32[]{:S(2)}) copy-start(s32[256]{0:T(256)} %param.15) | copy-start | bytes 3076
  3.3 150.5 %copy-start.1 = (s32[24]{0:T(128)S(1)}, s32[24]{0:T(128)}, u32[]{:S(2)}) copy-start(s32[24]{0:T(128)} %param.17) | copy-start | bytes 292
  3.3 150.5 %copy-start.2 = (s32[24]{0:T(128)S(1)}, s32[24]{0:T(128)}, u32[]{:S(2)}) copy-start(s32[24]{0:T(128)} %param.16) | copy-start | bytes 292
